TPU v7x, 128 devices: a whole 4x4x4 slice. The times are simulated.
128 devices in a mesh: chan: 64 (over x_lo, y, z, core), tm: 2 (over x_hi).
Axes of the slice: x: 4 (x_hi: 2, x_lo: 2; x = x_hi * 2 + x_lo), y: 4, z: 4, core: 2. Of those that a mesh axis runs over, the one named last changes fastest.
Arguments:
- voltages: bfloat16 [2048, 131840], P('chan', 'tm'), may hold values from -6 to 6
- kept: int32 [64], replicated, may hold values from 0 to 64, as said below
- assign: int32 [2048], replicated, may hold values from 0 to 2047, each once
Outputs:
- visibility: bfloat16 [64, 2048, 2, 2048], P('chan', 'tm')
Inputs may be any that keep to these rules, and one draw needn't show every extreme that they name: `kept`: distinct bins.
All inputs are finite; a program needn't handle non-finite values.
Results may differ from a plain program's by a relative error of at most 0.0062.
Values may be sent and summed in bfloat16 or wider, within the bound.
A program may use at most 192 MiB of HBM per device.

v0:
```python
import jax
import jax.numpy as jnp
from jax import lax
from jax.sharding import PartitionSpec as P

NFFT = 128
TAPS = 4
SPEC_DEV = 512


def filter_coeffs(kept, tap_count, points):
    length = tap_count * points
    places = jnp.arange(length, dtype=jnp.int32)
    positions = places.astype(jnp.float32)
    window = jnp.sinc((positions - (length - 1) / 2.0) / points) * (
        0.54 - 0.46 * jnp.cos(2.0 * jnp.pi * positions / (length - 1))
    )
    factor = 1.0 / jnp.sqrt(jnp.sum(window * window))
    phase_index = places[:, None] % points * kept[None, :] % points
    angles = 2.0 * jnp.pi * phase_index.astype(jnp.float32) / points
    paired = (
        jnp.stack([jnp.cos(angles), -jnp.sin(angles)], axis=2) * (window * factor)[:, None, None]
    )
    return paired.reshape(length, 2 * kept.shape[0]).astype(jnp.bfloat16)


def stacked(channel):
    lefthand = jnp.concatenate([channel[0], channel[1]], axis=1)
    flipped = jnp.concatenate([-channel[1], channel[0]], axis=1)
    return (lefthand, jnp.concatenate([lefthand, flipped], axis=0))


def products(upper_rows, lower_rows):
    return lax.dot_general(
        upper_rows, lower_rows, (((1,), (1,)), ((), ())), preferred_element_type=jnp.float32
    )


def shards(voltages, kept, assign):
    local_inputs = voltages.shape[0]
    channel_count = kept.shape[0]
    input_count = assign.shape[0]
    coeffs = filter_coeffs(kept, TAPS, NFFT)
    frames = voltages.reshape(local_inputs, SPEC_DEV + TAPS - 1, NFFT)
    summed = jnp.zeros((2 * channel_count, local_inputs, SPEC_DEV), jnp.float32)
    for tap_index in range(TAPS):
        summed = summed + jnp.einsum(
            "isn,nc->cis",
            frames[:, tap_index : tap_index + SPEC_DEV],
            coeffs[tap_index * NFFT : (tap_index + 1) * NFFT],
            preferred_element_type=jnp.float32,
        )
    local = summed.astype(jnp.bfloat16).reshape(channel_count, 2, local_inputs, SPEC_DEV)
    slot_of = (
        jnp.zeros((input_count,), jnp.int32)
        .at[assign]
        .set(jnp.arange(input_count, dtype=jnp.int32))
    )
    halves = lax.axis_size("tm")
    row_count = input_count // halves
    row_start = lax.axis_index("tm") * row_count
    factor = 1.0 / (SPEC_DEV * halves)
    turned = lax.all_to_all(local, "chan", split_axis=0, concat_axis=2, tiled=True)
    ordered = jnp.take(turned[0], slot_of, axis=1)
    lefthand, righthand = stacked(lax.all_gather(ordered, "tm", axis=2, tiled=True))
    upper_rows = lax.dynamic_slice_in_dim(lefthand, row_start, row_count, 0)
    visible = products(upper_rows, righthand)
    return (visible * factor).astype(jnp.bfloat16).reshape(1, row_count, 2, input_count)


def solution(mesh):
    placed = (P("chan", "tm"), P(), P())
    return jax.shard_map(
        shards, mesh=mesh, in_specs=placed, out_specs=P("chan", "tm", None, None), check_vma=False
    )
```

profile of v0, /device:TPU:1, one launch (start us, length us, event | category | flops | bytes accessed | tf_op | source)
XLA Modules:
  0.0 355.1 jit_solution(2094503597432644505)
XLA Ops:
  6.5 0.6 multiply_reduce_fusion
  7.2 1.2 fusion.26
  8.5 0.2 copy.15
  8.7 0.2 stack.8
  9.6 5.7 %reshape.204 = bf16[32,515,128]{2,1,0:T(8,128)(2,1)} reshape(bf16[32,65920]{1,0:T(8,128)(2,1)} %param.3) | data formatting | bytes 8437760 | tf_op jit(solution)/shard_map/reshape | solution.py:44
  15.3 0.0 slice-start
  15.3 0.0 slice-start.1
  15.3 6.9 %fusion.14 = f32[128,32,512]{2,0,1:T(8,128)} fusion(bf16[32,515,128]{2,1,0:T(8,128)(2,1)} %reshape.204, bf16[512,128]{0,1:T(8,128)(2,1)S(1)} %multiply_convert_fusion.1), kind=kOutput, calls=%fused_computation.18 | convolution fusion | flops 536870912 | bytes 12615680 | tf_op jit(solution)/shard_map/isn,nc->cis/dot_general | solution.py:47
  22.2 0.0 slice-done
  22.2 0.0 slice-done.1
  22.2 4.5 %fusion.16 = f32[128,32,512]{2,0,1:T(8,128)} fusion(bf16[32,515,128]{2,1,0:T(8,128)(2,1)S(1)} %bitcast.29, bf16[512,128]{0,1:T(8,128)(2,1)S(1)} %multiply_convert_fusion.1), kind=kOutput, calls=%fused_computation.20 | convolution fusion | flops 536870912 | bytes 12615680 | tf_op jit(solution)/shard_map/isn,nc->cis/dot_general | solution.py:47
  26.7 4.7 %fusion.12 = f32[128,32,512]{2,0,1:T(8,128)} fusion(bf16[32,515,128]{2,1,0:T(8,128)(2,1)S(1)} %bitcast.29, bf16[512,128]{0,1:T(8,128)(2,1)S(1)} %multiply_convert_fusion.1), kind=kOutput, calls=%fused_computation.16 | convolution fusion | flops 536870912 | bytes 12615680 | tf_op jit(solution)/shard_map/isn,nc->cis/dot_general | solution.py:47
  31.4 11.5 %add_convert_fusion = bf16[128,32,512]{2,0,1:T(8,128)(2,1)} fusion(f32[128,32,512]{2,0,1:T(8,128)} %fusion.12, f32[128,32,512]{2,0,1:T(8,128)} %fusion.14, f32[128,32,512]{2,0,1:T(8,128)} %fusion.16, bf16[32,515,128]{2,1,0:T(8,128)(2,1)S(1)} %bitcast.29, bf16[512,128]{0,1:T(8,128)(2,1)S(1)} %multiply_convert_fusion.1), kind=kOutput, calls=%fused_computation.13 | convolution fusion | flops 545259520 | bytes 33587200 | tf_op jit(solution)/shard_map/isn,nc->cis/dot_general | solution.py:47
  42.9 6.5 %copy.19 = bf16[128,32,512]{2,1,0:T(8,128)(2,1)} copy(bf16[128,32,512]{2,0,1:T(8,128)(2,1)} %add_convert_fusion) | data formatting | bytes 8388608 | tf_op jit(solution)/shard_map/reshape | solution.py:53
  49.4 0.0 copy-start
  49.4 11.2 %all-to-all-start = ((bf16[64,2,32,512]{3,2,1,0:T(8,128)(2,1)}), bf16[64,2,32,512]{3,2,1,0:T(8,128)(2,1)}, u32[]{:S(2)}, u32[]{:S(2)}) async-start(bf16[64,2,32,512]{3,2,1,0:T(8,128)(2,1)} %bitcast.30), calls=%async_computation | async-start | bytes 8388608 | tf_op jit(solution)/shard_map/all_to_all | solution.py:63
  60.7 0.0 all-gather.2.cloned.1.call-start
  60.7 0.0 copy-done
  60.8 8.2 %scatter_custom_fusion = s32[2048]{0:T(1024)S(1)} fusion(s32[2048]{0:T(1024)S(1)} %compare_select_fusion.1, s32[2048]{0:T(1024)S(1)} %iota.14, s32[]{:T(128)} %constant.62.clone.1), kind=kCustom, calls=%fused_computation.47 | custom fusion | bytes 8196 | tf_op jit(solution)/shard_map/scatter | solution.py:57
  69.0 44.0 %all-to-all-done = bf16[64,2,32,512]{3,2,1,0:T(8,128)(2,1)} async-done(((bf16[64,2,32,512]{3,2,1,0:T(8,128)(2,1)}), bf16[64,2,32,512]{3,2,1,0:T(8,128)(2,1)}, u32[]{:S(2)}, u32[]{:S(2)}) %all-to-all-start) | async-done | bytes 4194336 | tf_op jit(solution)/shard_map/all_to_all | solution.py:63
  113.0 2.7 copy.17
  115.7 19.0 %copy.18 = bf16[2,2048,512]{2,0,1:T(2,128)(2,1)} copy(bf16[2,2048,512]{2,1,0:T(8,128)(2,1)S(1)} %bitcast.31) | data formatting | bytes 8388608 | tf_op jit(solution)/shard_map/squeeze | solution.py:64
  134.8 23.6 %gather_fusion = bf16[2048,2,512]{2,1,0:T(2,128)(2,1)} fusion(bf16[2,2048,512]{2,0,1:T(2,128)(2,1)} %copy.18, s32[2048]{0:T(1024)S(1)} %fusion.27), kind=kCustom, calls=%fused_computation | custom fusion | bytes 8396800 | tf_op jit(solution)/shard_map/jit(_take)/gather | solution.py:64
  158.3 9.3 %fusion.20 = bf16[2,2048,512]{2,0,1:T(2,128)(2,1)} fusion(bf16[2048,2,512]{2,1,0:T(2,128)(2,1)} %gather_fusion, pred[2048]{0:T(1024)(128)(4,1)S(1)} %compare_and_fusion), kind=kLoop, calls=%fused_computation.26 | loop fusion | flops 2097152 | bytes 8390656 | tf_op jit(solution)/shard_map/jit(_take)/select_n | solution.py:64
  167.6 0.0 all-gather.2.cloned.1.call-update
  167.6 108.5 %all-gather.2.cloned.1.call-done = bf16[2,2048,1024]{2,0,1:T(2,128)(2,1)} async-done(((bf16[2,2048,512]{2,0,1:T(2,128)(2,1)}), bf16[2,2048,1024]{2,0,1:T(2,128)(2,1)}) %all-gather.2.cloned.1.call-update) | async-done | bytes 8388624 | tf_op jit(solution)/shard_map/all_gather | solution.py:65
  276.1 17.1 %fusion.47 = (bf16[1,2048,1024]{2,0,1:T(2,128)(2,1)}, bf16[1,2048,1024]{2,0,1:T(2,128)(2,1)S(1)}) fusion(bf16[2,2048,1024]{2,0,1:T(2,128)(2,1)} %all-gather.2.cloned.1.call-done), kind=kLoop, calls=%fused_computation.82 | loop fusion | bytes 16777216 | tf_op jit(solution)/shard_map/slice | solution.py:28
  293.2 8.1 %fusion.46 = (bf16[2048,1024]{1,0:T(8,128)(2,1)}, bf16[2048,1024]{1,0:T(8,128)(2,1)}) fusion(bf16[1,2048,1024]{2,0,1:T(2,128)(2,1)} %get-tuple-element.7), kind=kLoop, calls=%fused_computation.81 | loop fusion | flops 2097152 | bytes 12582912 | tf_op jit(solution)/shard_map/neg | solution.py:29
  301.3 3.7 %copy.25 = bf16[1,2048,1024]{2,1,0:T(8,128)(2,1)} copy(bf16[1,2048,1024]{2,0,1:T(2,128)(2,1)S(1)} %get-tuple-element.8) | data formatting | bytes 8388608
  305.0 28.8 %multiply_convert_fusion = bf16[1024,4096]{1,0:T(8,128)(2,1)} fusion(bf16[2048,1024]{1,0:T(8,128)(2,1)} %bitcast.32, bf16[2048,1024]{1,0:T(8,128)(2,1)} %get-tuple-element.5, bf16[2048,1024]{1,0:T(8,128)(2,1)} %get-tuple-element.6, s32[]{:T(128)S(6)} %select_n.106), kind=kOutput, calls=%fused_computation.10 | convolution fusion | flops 17263755264 | bytes 29360132 | tf_op jit(solution)/shard_map/dot_general | solution.py:34
  333.9 14.4 %reshape.206 = bf16[1,1024,2,2048]{3,2,1,0:T(2,128)(2,1)} reshape(bf16[1024,4096]{1,0:T(8,128)(2,1)} %multiply_convert_fusion) | data formatting | bytes 16777216 | tf_op jit(solution)/shard_map/reshape | solution.py:68
  (9 shorter events, 0.1 us)
Async XLA Ops:
  15.3 6.9 %slice-start = ((s8[4259840]{0:T(1024)(128)(4,1)}), s8[4194304]{0:T(1024)(128)(4,1)S(1)}, s32[]{:S(2)}) async-start(s8[4259840]{0:T(1024)(128)(4,1)} %bitcast.28), calls=%async_computation.2 | async-start | bytes 8388608
  15.3 6.9 %slice-start.1 = ((s8[4259840]{0:T(1024)(128)(4,1)}), s8[65536]{0:T(1024)(128)(4,1)S(1)}, s32[]{:S(2)}) async-start(s8[4259840]{0:T(1024)(128)(4,1)} %bitcast.28), calls=%async_computation.3 | async-start | bytes 131072
  49.4 11.3 %copy-start = (s32[2048]{0:T(1024)S(1)}, s32[2048]{0:T(1024)}, u32[]{:S(2)}) copy-start(s32[2048]{0:T(1024)} %param.5) | copy-start | bytes 24580
  49.4 63.6 %all-to-all-start = ((bf16[64,2,32,512]{3,2,1,0:T(8,128)(2,1)}), bf16[64,2,32,512]{3,2,1,0:T(8,128)(2,1)}, u32[]{:S(2)}, u32[]{:S(2)}) async-start(bf16[64,2,32,512]{3,2,1,0:T(8,128)(2,1)} %bitcast.30), calls=%async_computation | async-start | bytes 8388608 | tf_op jit(solution)/shard_map/all_to_all | solution.py:63
  60.7 215.4 %all-gather.2.cloned.1.call-start = ((), (), s32[]{:S(2)}) async-start(), calls=%async_computation.1 | async-start | bytes 12582912 | tf_op jit(solution)/shard_map/all_gather | solution.py:65
Sparse Core Ops, SparseCore 0:
  167.7 108.3 all-gather.1
where the time goes:
time: 356 us; the launch traced here: 355 us
  waiting for transfers between devices  152 us (43%)
  local copies, waits for them, and re-layouts  101 us (28%)
  matrix products  56.4 us (16%)
  other arithmetic  19.4 us (5%)
  between operations  14.2 us (4%)
  starting transfers between devices  11.3 us (3%)
    all_gather x1, waiting for transfers between devices, shards(): lax.all_gather(ordered, 'tm', axis=2, tiled=True)  108 us
    all_to_all x1, waiting for transfers between devices, shards(): lax.all_to_all(local, 'chan', split_axis=0, concat_axis=2, tiled=True)  44 us
    dot_general x1, matrix products, products(): lax.dot_general(upper_rows, lower_rows, (((1,), (1,)), ((), ())), preferr...  28.8 us
    dot_general x4, matrix products, shards(): jnp.einsum('isn,nc->cis', frames[:, tap_index:tap_index + SPEC_DEV], coef...  27.6 us
    gather x1, local copies, waits for them, and re-layouts, shards(): ordered = jnp.take(turned[0], slot_of, axis=1)  23.6 us
    squeeze x1, local copies, waits for them, and re-layouts, shards(): ordered = jnp.take(turned[0], slot_of, axis=1)  19 us
    slice x1, local copies, waits for them, and re-layouts, stacked(): lefthand = jnp.concatenate([channel[0], channel[1]], axis=1)  17.1 us
    reshape x1, local copies, waits for them, and re-layouts, shards(): (visible * factor).astype(jnp.bfloat16)  14.4 us
  transfers between devices with their start and end apart: 2, of which 2 were waited for; matrix products, arithmetic and copies ran while one was open for 2% of the time, Pallas kernels for 0%

commit v1 on v0

v1 whole, which is shorter than its diff:
```python
import jax
import jax.numpy as jnp
import numpy as np
from jax import lax
from jax.experimental import pallas as pl
from jax.experimental.pallas import tpu as pltpu
from jax.sharding import PartitionSpec as P

NFFT = 128
TAPS = 4
SPEC_DEV = 512
SAMP_DEV = 65920
INPUTS = 2048
CHANNELS = 64
ROWS = 1024
LOCAL = 32
PARTS = 4
CHUNK = SPEC_DEV // PARTS
WIDE = 2 * CHUNK
MESH = pl.DeviceIdType.MESH
BF = jnp.bfloat16
F32 = jnp.float32


def coefficients(kept):
    length = TAPS * NFFT
    at = np.arange(length, dtype=np.float64)
    window = np.sinc((at - (length - 1) / 2.0) / NFFT) * (
        0.54 - 0.46 * np.cos(2.0 * np.pi * at / (length - 1))
    )
    window = jnp.asarray(window / np.sqrt(np.sum(window * window)), F32)
    places = jnp.arange(length, dtype=jnp.int32) % NFFT
    quarter = jnp.array([0, NFFT // 4], jnp.int32)
    turns = (places[None, None, :] * kept[None, :, None] + quarter[:, None, None]) % NFFT
    angles = turns.astype(F32) * (2.0 * np.pi / NFFT)
    return (jnp.cos(angles) * window).astype(BF).reshape(2 * CHANNELS, length)


def contract_lanes(left, right):
    return lax.dot_general(left, right, (((1,), (1,)), ((), ())), preferred_element_type=F32)


def dot(left, right):
    return jnp.dot(left, right, preferred_element_type=F32)


def main_kernel(
    volt_hbm,
    coef,
    assign,
    out_hbm,
    volt,
    perm,
    frames,
    chan,
    sendbuf,
    near,
    slab_a,
    slab_b,
    slab_c,
    onehot,
    right,
    left,
    acc,
    stage,
    volt_sem,
    near_send,
    near_recv,
    slab_send,
    slab_recv,
    out_sem,
):
    me = lax.axis_index("chan")
    half = lax.axis_index("tm")
    low = me // 32
    y = (me // 8) % 4
    z = (me // 2) % 4
    core = me % 2
    place = me % 32

    def volt_copy(q):
        first = 0 if q == 0 else (q * CHUNK + 3) * NFFT
        last = ((q + 1) * CHUNK + 3) * NFFT
        part = pl.ds(first, last - first)
        return pltpu.make_async_copy(volt_hbm.at[:, part], volt.at[:, part], volt_sem.at[q])

    for q in range(PARTS):
        volt_copy(q).start()

    def near_device(dy, dz, dc):
        there = (((y + dy) % 4) * 4 + (z + dz) % 4) * 2 + (core + dc) % 2
        return there

    barrier = pltpu.get_barrier_semaphore()

    def greet(k, carry):
        there = near_device(k // 8, (k // 2) % 4, k % 2)
        pl.semaphore_signal(
            barrier, inc=1, device_id=(low * 32 + there, half), device_id_type=MESH
        )
        return carry

    lax.fori_loop(1, 32, greet, 0)
    far = (
        ((1 - low) * 32 + place, half),
        ((1 - low) * 32 + place, 1 - half),
        (low * 32 + place, 1 - half),
    )
    for device in far:
        pl.semaphore_signal(barrier, inc=1, device_id=device, device_id_type=MESH)

    row = lax.broadcasted_iota(jnp.int32, (256, 256), 0)
    col = lax.broadcasted_iota(jnp.int32, (256, 256), 1)
    perm[...] = jnp.where(col == (row & 15) * 16 + (row >> 4), 1.0, 0.0).astype(BF)

    def channelize(q):
        volt_copy(q).wait()
        for ih in range(2):

            def reorder(sb, carry):
                base = (q * CHUNK + sb * 16) * NFFT
                pieces = [
                    volt[ih * 16 : ih * 16 + 16, pl.ds(pl.multiple_of(base + s * NFFT, NFFT), 4 * NFFT)]
                    for s in range(16)
                ]
                moved = dot(perm[...], jnp.concatenate(pieces, axis=0)).astype(BF)
                frames[:, pl.ds(pl.multiple_of(sb * 16, 16), 16), :] = moved.reshape(16, 16, 4 * NFFT)
                return carry

            lax.fori_loop(0, CHUNK // 16, reorder, 0)

            def transform(ip, carry):
                pair = frames[pl.ds(ip * 2, 2)].reshape(2 * CHUNK, 4 * NFFT)
                found = contract_lanes(coef[...], pair).astype(BF)
                for i in range(2):
                    for p in range(2):
                        chan[ip * 2 + i, :, p * CHUNK : (p + 1) * CHUNK] = found[
                            p * CHANNELS : (p + 1) * CHANNELS, i * CHUNK : (i + 1) * CHUNK
                        ]
                return carry

            lax.fori_loop(0, 8, transform, 0)

            for cb in range(4):
                block = chan[:, cb * 16 : cb * 16 + 16, :].reshape(256, WIDE)
                moved = dot(perm[...], block).astype(BF).reshape(16, 16, WIDE)
                sendbuf[q, cb // 2, (cb % 2) * 16 : (cb % 2) * 16 + 16, ih * 16 : ih * 16 + 16, :] = moved

    my_rows = pl.ds(pl.multiple_of(place * LOCAL, LOCAL), LOCAL)

    def self_copy(q):
        return pltpu.make_async_copy(
            sendbuf.at[q, :, place], near.at[q, :, my_rows], near_recv.at[q, y]
        )

    def near_copy(q, dy, dz, dc):
        there = near_device(dy, dz, dc)
        return pltpu.make_async_remote_copy(
            src_ref=sendbuf.at[q, :, there],
            dst_ref=near.at[q, :, my_rows],
            send_sem=near_send.at[q],
            recv_sem=near_recv.at[q, y],
            device_id=(low * 32 + there, half),
            device_id_type=MESH,
        )

    def send_near(q):
        self_copy(q).start()
        if q == 0:

            def first(k, carry):
                near_copy(q, 0, k // 2, k % 2).start()
                return carry

            lax.fori_loop(1, 8, first, 0)

            def second(k, carry):
                near_copy(q, 1 + 2 * (k % 2), (k // 2) % 4, k // 8).start()
                return carry

            lax.fori_loop(0, 16, second, 0)

            def third(k, carry):
                near_copy(q, 2, k // 2, k % 2).start()
                return carry

            lax.fori_loop(0, 8, third, 0)
        else:

            def some(k, carry):
                o = (k * 11) % 32
                near_copy(q, o % 4, (o // 4) % 4, o // 16).start()
                return carry

            lax.fori_loop(1, 32, some, 0)

    def slab_copy(q, group, kind):
        rows = pl.ds(pl.multiple_of(group * 256, 256), 256)
        which = low if kind == 2 else 1 - low
        slab = (slab_a, slab_b, slab_c)[kind]
        return pltpu.make_async_remote_copy(
            src_ref=near.at[q, which, rows],
            dst_ref=slab.at[q, rows],
            send_sem=slab_send.at[q],
            recv_sem=slab_recv.at[q, kind],
            device_id=far[kind],
            device_id_type=MESH,
        )

    def wait_group(q, group):
        rows = pl.ds(pl.multiple_of(group * 256, 256), 256)
        block = near.at[q, :, rows]
        pltpu.make_async_copy(block, block, near_recv.at[q, group]).wait()

    def forward_group(q, step):
        group = (y + (0, 1, 3, 2)[step]) % 4
        wait_group(q, group)
        for kind in range(3):
            slab_copy(q, group, kind).start()

    def forward(q):
        for step in range(4):
            wait_group(q, (y + step) % 4)
        for step in range(4):
            for kind in range(2):
                slab_copy(q, step, kind).start()
        for step in range(4):
            slab_copy(q, step, 2).start()

    def wait_slab(q, kind):
        block = (slab_a, slab_b, slab_c)[kind].at[q]
        pltpu.make_async_copy(block, block, slab_recv.at[q, kind]).wait()

    def reorder_inputs(mine, other):
        def part(t, carry):
            rows = pl.ds(pl.multiple_of(t * 512, 512), 512)
            total = dot(onehot[low, rows, :], mine[...]) + dot(onehot[1 - low, rows, :], other[...])
            right[rows, :] = total.astype(BF)
            return carry

        lax.fori_loop(0, INPUTS // 512, part, 0)

        def take(t, carry):
            rows = pl.ds(pl.multiple_of(half * ROWS + t * 256, 256), 256)
            block = right[rows, :]
            upper = pl.ds(pl.multiple_of(t * 256, 256), 256)
            lower = pl.ds(pl.multiple_of(ROWS + t * 256, 256), 256)
            left[upper, :] = block
            left[lower, :CHUNK] = block[:, CHUNK:]
            left[lower, CHUNK:] = -block[:, :CHUNK]
            return carry

        lax.fori_loop(0, ROWS // 256, take, 0)

    def correlate():
        def tile(n, carry):
            columns = right[pl.ds(pl.multiple_of(n * 256, 256), 256), :]
            for m in range(4):
                rows = slice(m * 512, (m + 1) * 512)
                acc[n, rows, :] += contract_lanes(left[rows, :], columns)
            return carry

        lax.fori_loop(0, 8, tile, 0)

    def out_copy(n, slot):
        columns = pl.ds(pl.multiple_of(n * 256, 256), 256)
        return pltpu.make_async_copy(stage.at[slot], out_hbm.at[:, columns], out_sem.at[slot])

    def finish():
        def tile(n, carry):
            slot = n % 2

            @pl.when(n >= 2)
            def _():
                out_copy(n - 2, slot).wait()

            columns = right[pl.ds(pl.multiple_of(n * 256, 256), 256), :]
            for m in range(4):
                rows = slice(m * 512, (m + 1) * 512)
                total = acc[n, rows, :] + contract_lanes(left[rows, :], columns)
                stage[slot, rows, :] = (total * (1.0 / 1024.0)).astype(BF)
            out_copy(n, slot).start()
            return carry

        lax.fori_loop(0, 8, tile, 0)
        out_copy(6, 0).wait()
        out_copy(7, 1).wait()

    def own_half(q):
        wait_slab(q, 0)
        reorder_inputs(near.at[q, low], slab_a.at[q])

    def other_half(q):
        wait_slab(q, 1)
        wait_slab(q, 2)
        reorder_inputs(slab_c.at[q], slab_b.at[q])

    channelize(0)
    pl.semaphore_wait(barrier, 34)
    send_near(0)
    forward_group(0, 0)
    channelize(1)
    send_near(1)
    for step in range(1, 4):
        forward_group(0, step)
    channelize(2)
    send_near(2)
    channelize(3)
    send_near(3)

    def fill(t, carry):
        rows = pl.ds(pl.multiple_of(t * 256, 256), 256)
        antenna = t * 256 + lax.broadcasted_iota(jnp.int32, (256, ROWS), 0)
        for s in range(2):
            same = antenna == assign[:, s * ROWS : (s + 1) * ROWS]
            onehot[s, rows, :] = jnp.where(same, 1.0, 0.0).astype(BF)
        acc[t] = jnp.zeros((INPUTS, 256), F32)
        return carry

    lax.fori_loop(0, 8, fill, 0)
    forward(1)
    own_half(0)
    correlate()
    other_half(0)
    correlate()
    forward(2)
    forward(3)

    def middle(q, carry):
        own_half(q)
        correlate()
        other_half(q)
        correlate()
        return carry

    lax.fori_loop(1, 3, middle, 0)
    own_half(3)
    correlate()
    other_half(3)
    finish()

    for q in range(PARTS):
        sent = sendbuf.at[q, :, pl.ds(0, 31)]
        pltpu.make_async_copy(sent, sent, near_send.at[q]).wait()
        for slab in (slab_a, slab_b, slab_c):
            pltpu.make_async_copy(slab.at[q], slab.at[q], slab_send.at[q]).wait()


def place_kernel(perm, x, o):
    def body(g, carry):
        rows = pl.ds(pl.multiple_of(g * 16, 16), 16)
        for jh in range(2):
            parts = [
                x[p, rows, (jh * 8 + j) * 128 : (jh * 8 + j + 1) * 128]
                for j in range(8)
                for p in range(2)
            ]
            moved = dot(perm[...], jnp.concatenate(parts, axis=0)).astype(BF)
            o[rows, jh * 16 : (jh + 1) * 16, :] = moved.reshape(16, 16, 128)
        return carry

    lax.fori_loop(0, x.shape[1] // 16, body, 0)


def shards(voltages, kept, assign):
    coef = coefficients(kept)
    dma = pltpu.SemaphoreType.DMA
    vmem = pl.BlockSpec(memory_space=pltpu.VMEM)
    hbm = pl.BlockSpec(memory_space=pl.ANY)
    found = pl.pallas_call(
        main_kernel,
        out_shape=jax.ShapeDtypeStruct((2 * ROWS, INPUTS), BF),
        in_specs=[hbm, vmem, vmem],
        out_specs=hbm,
        scratch_shapes=[
            pltpu.VMEM((LOCAL, SAMP_DEV), BF),
            pltpu.VMEM((256, 256), BF),
            pltpu.VMEM((16, CHUNK, 4 * NFFT), BF),
            pltpu.VMEM((16, CHANNELS, WIDE), BF),
            pltpu.VMEM((PARTS, 2, 32, LOCAL, WIDE), BF),
            pltpu.VMEM((PARTS, 2, ROWS, WIDE), BF),
            pltpu.VMEM((PARTS, ROWS, WIDE), BF),
            pltpu.VMEM((PARTS, ROWS, WIDE), BF),
            pltpu.VMEM((PARTS, ROWS, WIDE), BF),
            pltpu.VMEM((2, INPUTS, ROWS), BF),
            pltpu.VMEM((INPUTS, WIDE), BF),
            pltpu.VMEM((2 * ROWS, WIDE), BF),
            pltpu.VMEM((8, 2 * ROWS, 256), F32),
            pltpu.VMEM((2, 2 * ROWS, 256), BF),
            dma((PARTS,)),
            dma((PARTS,)),
            dma((PARTS, 4)),
            dma((PARTS,)),
            dma((PARTS, 3)),
            dma((2,)),
        ],
        compiler_params=pltpu.CompilerParams(
            collective_id=0, has_side_effects=True, vmem_limit_bytes=60 << 20
        ),
        name="exchange_correlate",
    )(voltages, coef, assign.reshape(1, INPUTS))

    r = np.arange(256)
    source = ((r % 16) // 2) * 32 + (r % 2) * 16 + r // 16
    perm = jnp.asarray(source[:, None] == r[None, :], BF)
    tile = 128
    placed = pl.pallas_call(
        place_kernel,
        grid=(ROWS // tile,),
        in_specs=[
            pl.BlockSpec((256, 256), lambda i: (0, 0)),
            pl.BlockSpec((2, tile, INPUTS), lambda i: (0, i, 0)),
        ],
        out_specs=pl.BlockSpec((tile, 32, 128), lambda i: (i, 0, 0)),
        out_shape=jax.ShapeDtypeStruct((ROWS, 32, 128), BF),
        compiler_params=pltpu.CompilerParams(vmem_limit_bytes=16 << 20),
        name="place",
    )(perm, found.reshape(2, ROWS, INPUTS))
    return placed.reshape(ROWS, 16, 2, 128).transpose(0, 2, 1, 3).reshape(1, ROWS, 2, INPUTS)


def solution(mesh):
    placed = (P("chan", "tm"), P(), P())
    return jax.shard_map(
        shards, mesh=mesh, in_specs=placed, out_specs=P("chan", "tm", None, None), check_vma=False
    )
```

time: 356 us -> 160 us (0.45)
  waiting for transfers between devices: 152 us -> 0 us
  Pallas kernels: 0 us -> 151 us
  local copies, waits for them, and re-layouts: 101 us -> 3.54 us
  matrix products: 56.4 us -> 0 us
  other arithmetic: 19.4 us -> 3.12 us
  between operations: 14.2 us -> 0.04 us
  starting transfers between devices: 11.3 us -> 0 us
    pallas_call x0 -> x2, Pallas kernels: none -> 151 us  [the longest x1 135 us: shards(): pl.pallas_call(main_kernel, out_shape=jax.ShapeDtypeStruct((2 * ROWS, INP...]
    all_gather x1 -> x0, waiting for transfers between devices: 108 us -> none  [shards(): lax.all_gather(ordered, 'tm', axis=2, tiled=True)]
    dot_general x5 -> x0, matrix products: 56.4 us -> none  [the longest x1 28.8 us: products(): lax.dot_general(upper_rows, lower_rows, (((1,), (1,)), ((), ())), preferr...]
    all_to_all x1 -> x0, waiting for transfers between devices: 44 us -> none  [shards(): lax.all_to_all(local, 'chan', split_axis=0, concat_axis=2, tiled=True)]
    reshape x3 -> x0, local copies, waits for them, and re-layouts: 26.7 us -> none  [the longest x1 14.4 us: shards(): (visible * factor).astype(jnp.bfloat16)]
    gather x1 -> x0, local copies, waits for them, and re-layouts: 23.6 us -> none  [shards(): ordered = jnp.take(turned[0], slot_of, axis=1)]
    squeeze x1 -> x0, local copies, waits for them, and re-layouts: 19 us -> none  [shards(): ordered = jnp.take(turned[0], slot_of, axis=1)]
    slice x1 -> x0, local copies, waits for them, and re-layouts: 17.1 us -> none  [stacked(): lefthand = jnp.concatenate([channel[0], channel[1]], axis=1)]
  transfers between devices with their start and end apart: 2 -> 0, of which waited for: 2 -> 0; matrix products, arithmetic and copies ran while one was open for 2% -> 0% of each run, Pallas kernels for 0% -> 0%
where the time goes in v1:
time: 160 us; the launch traced here: 158 us
  Pallas kernels  151 us (94%)
  local copies, waits for them, and re-layouts  3.54 us (2%)
  other arithmetic  3.12 us (2%)
    pallas_call x1, Pallas kernels, shards(): pl.pallas_call(main_kernel, out_shape=jax.ShapeDtypeStruct((2 * ROWS, INP...  135 us
    pallas_call x1, Pallas kernels, shards(): pl.pallas_call(place_kernel, grid=(ROWS // tile,), in_specs=[pl.BlockSpec...  15.7 us
    unnamed x4, local copies, waits for them, and re-layouts  3.38 us

profile of v1, /device:TPU:1, one launch (start us, length us, event | category | flops | bytes accessed | tf_op | source)
XLA Modules:
  0.0 157.6 jit_solution(16727236421591425813)
XLA Ops:
  0.0 0.0 copy-start.1
  0.0 0.1 add.40
  0.1 0.1 add.41
  0.2 0.7 broadcast_multiply_fusion
  0.9 2.4 %fusion.5.coef = bf16[128,512]{1,0:T(8,128)(2,1)} fusion(f32[512]{0:T(512)} %constant.33.clone, s32[128]{0:T(128)S(1)} %add.41, s32[64,512]{1,0:T(8,128)S(1)} %broadcast_multiply_fusion), kind=kLoop, calls=%fused_computation.8 | loop fusion | flops 1048576 | bytes 264704 | tf_op jit(solution)/shard_map/convert_element_type | solution.py:36
  3.3 135.2 %exchange_correlate.1 = bf16[2048,2048]{1,0:T(8,128)(2,1)} custom-call(bf16[32,65920]{1,0:T(8,128)(2,1)} %volt_hbm.1, bf16[128,512]{1,0:T(8,128)(2,1)} %fusion.5.coef, s32[1,2048]{1,0:T(1,128)} %bitcast.24), custom_call_target="tpu_custom_call" | custom-call | tf_op jit(solution)/shard_map/exchange_correlate/pallas_call | solution.py:370
  138.5 0.0 copy-done.1
  138.5 0.0 copy-start
  138.5 3.4 %copy-done = bf16[2048,2048]{1,0:T(8,128)(2,1)S(1)} copy-done((bf16[2048,2048]{1,0:T(8,128)(2,1)S(1)}, bf16[2048,2048]{1,0:T(8,128)(2,1)}, u32[]{:S(2)}) %copy-start) | copy-done | bytes 8388632
  141.9 15.7 %place.1 = bf16[1024,32,128]{2,1,0:T(8,128)(2,1)} custom-call(bf16[256,256]{1,0:T(8,128)(2,1)S(1)} %copy-done.1, bf16[2,1024,2048]{2,1,0:T(8,128)(2,1)S(1)} %bitcast.23), custom_call_target="tpu_custom_call" | custom-call | tf_op jit(solution)/shard_map/place/pallas_call | solution.py:407
  (2 shorter events, 0.0 us)
Async XLA Ops:
  0.0 138.5 %copy-start.1 = (bf16[256,256]{1,0:T(8,128)(2,1)S(1)}, bf16[256,256]{1,0:T(8,128)(2,1)}, u32[]{:S(2)}) copy-start(bf16[256,256]{1,0:T(8,128)(2,1)} %constant.35.clone.perm) | copy-start | bytes 393220
  138.5 3.4 %copy-start = (bf16[2048,2048]{1,0:T(8,128)(2,1)S(1)}, bf16[2048,2048]{1,0:T(8,128)(2,1)}, u32[]{:S(2)}) copy-start(bf16[2048,2048]{1,0:T(8,128)(2,1)} %exchange_correlate.1) | copy-start | bytes 25165828

commit v2 on v1

--- a/solution.py
+++ b/solution.py
@@ -12,6 +12,7 @@
 SAMP_DEV = 65920
 INPUTS = 2048
 CHANNELS = 64
+TOTAL_SPEC = 1024
 ROWS = 1024
 LOCAL = 32
 PARTS = 4
@@ -22,18 +23,11 @@
 F32 = jnp.float32
 
 
-def coefficients(kept):
-    length = TAPS * NFFT
-    at = np.arange(length, dtype=np.float64)
-    window = np.sinc((at - (length - 1) / 2.0) / NFFT) * (
-        0.54 - 0.46 * np.cos(2.0 * np.pi * at / (length - 1))
-    )
-    window = jnp.asarray(window / np.sqrt(np.sum(window * window)), F32)
-    places = jnp.arange(length, dtype=jnp.int32) % NFFT
-    quarter = jnp.array([0, NFFT // 4], jnp.int32)
-    turns = (places[None, None, :] * kept[None, :, None] + quarter[:, None, None]) % NFFT
-    angles = turns.astype(F32) * (2.0 * np.pi / NFFT)
-    return (jnp.cos(angles) * window).astype(BF).reshape(2 * CHANNELS, length)
+def filter_window():
+    at = np.arange(TAPS * NFFT, dtype=np.float64)
+    middle = (TAPS * NFFT - 1) / 2.0
+    window = np.sinc((at - middle) / NFFT) * (0.54 - 0.46 * np.cos(np.pi * at / middle))
+    return (window / np.sqrt(np.sum(window * window)))[None, :]
 
 
 def contract_lanes(left, right):
@@ -46,11 +40,14 @@
 
 def main_kernel(
     volt_hbm,
-    coef,
+    kept,
+    window,
     assign,
-    out_hbm,
+    acc,
+    right,
     volt,
     perm,
+    coef,
     frames,
     chan,
     sendbuf,
@@ -59,16 +56,13 @@
     slab_b,
     slab_c,
     onehot,
-    right,
-    left,
-    acc,
-    stage,
+    lower,
+    partial,
     volt_sem,
     near_send,
     near_recv,
     slab_send,
     slab_recv,
-    out_sem,
 ):
     me = lax.axis_index("chan")
     half = lax.axis_index("tm")
@@ -113,6 +107,19 @@
     col = lax.broadcasted_iota(jnp.int32, (256, 256), 1)
     perm[...] = jnp.where(col == (row & 15) * 16 + (row >> 4), 1.0, 0.0).astype(BF)
 
+    bins = kept[...].astype(F32)
+    row = lax.broadcasted_iota(jnp.int32, (2 * CHANNELS, CHANNELS), 0)
+    col = lax.broadcasted_iota(jnp.int32, (2 * CHANNELS, CHANNELS), 1)
+    own_bin = jnp.sum(jnp.where((row & 63) == col, bins, 0.0), axis=1, keepdims=True)
+    row = lax.broadcasted_iota(jnp.int32, (2 * CHANNELS, NFFT), 0)
+    col = lax.broadcasted_iota(jnp.int32, (2 * CHANNELS, NFFT), 1)
+    turns = col.astype(F32) * own_bin + (row >> 6).astype(F32) * (NFFT / 4.0)
+    turns = turns - jnp.floor(turns * (1.0 / NFFT)) * NFFT
+    wave = jnp.cos(turns * (2.0 * np.pi / NFFT))
+    for tap in range(TAPS):
+        lanes = slice(tap * NFFT, (tap + 1) * NFFT)
+        coef[:, lanes] = (wave * window[:, lanes]).astype(BF)
+
     def channelize(q):
         volt_copy(q).wait()
         for ih in range(2):
@@ -127,7 +134,7 @@
                 frames[:, pl.ds(pl.multiple_of(sb * 16, 16), 16), :] = moved.reshape(16, 16, 4 * NFFT)
                 return carry
 
-            lax.fori_loop(0, CHUNK // 16, reorder, 0)
+            lax.fori_loop(0, CHUNK // 16, reorder, 0, unroll=True)
 
             def transform(ip, carry):
                 pair = frames[pl.ds(ip * 2, 2)].reshape(2 * CHUNK, 4 * NFFT)
@@ -139,7 +146,7 @@
                         ]
                 return carry
 
-            lax.fori_loop(0, 8, transform, 0)
+            lax.fori_loop(0, 8, transform, 0, unroll=True)
 
             for cb in range(4):
                 block = chan[:, cb * 16 : cb * 16 + 16, :].reshape(256, WIDE)
@@ -233,58 +240,51 @@
 
     def reorder_inputs(mine, other):
         def part(t, carry):
-            rows = pl.ds(pl.multiple_of(t * 512, 512), 512)
+            rows = pl.ds(pl.multiple_of(t * 1024, 1024), 1024)
             total = dot(onehot[low, rows, :], mine[...]) + dot(onehot[1 - low, rows, :], other[...])
             right[rows, :] = total.astype(BF)
             return carry
 
-        lax.fori_loop(0, INPUTS // 512, part, 0)
-
-        def take(t, carry):
-            rows = pl.ds(pl.multiple_of(half * ROWS + t * 256, 256), 256)
-            block = right[rows, :]
-            upper = pl.ds(pl.multiple_of(t * 256, 256), 256)
-            lower = pl.ds(pl.multiple_of(ROWS + t * 256, 256), 256)
-            left[upper, :] = block
-            left[lower, :CHUNK] = block[:, CHUNK:]
-            left[lower, CHUNK:] = -block[:, :CHUNK]
+        lax.fori_loop(0, 2, part, 0)
+
+    def reorder_first(other):
+        def part(t, carry):
+            rows = pl.ds(pl.multiple_of(t * 1024, 1024), 1024)
+            partial[rows, :] = dot(onehot[1 - low, rows, :], other[...])
             return carry
 
-        lax.fori_loop(0, ROWS // 256, take, 0)
-
-    def correlate():
+        lax.fori_loop(0, 2, part, 0)
+
+    def reorder_second(mine):
+        def part(t, carry):
+            rows = pl.ds(pl.multiple_of(t * 1024, 1024), 1024)
+            total = partial[rows, :] + dot(onehot[low, rows, :], mine[...])
+            right[rows, :] = total.astype(BF)
+            return carry
+
+        lax.fori_loop(0, 2, part, 0)
+
+    def correlate(first=False):
+        for t in range(4):
+            block = right[pl.ds(pl.multiple_of(half * ROWS + t * 256, 256), 256), :]
+            lower[t * 256 : (t + 1) * 256, :CHUNK] = block[:, CHUNK:]
+            lower[t * 256 : (t + 1) * 256, CHUNK:] = -block[:, :CHUNK]
+
         def tile(n, carry):
-            columns = right[pl.ds(pl.multiple_of(n * 256, 256), 256), :]
-            for m in range(4):
-                rows = slice(m * 512, (m + 1) * 512)
-                acc[n, rows, :] += contract_lanes(left[rows, :], columns)
+            columns = right[pl.ds(pl.multiple_of(n * ROWS, ROWS), ROWS), :]
+            for m in range(8):
+                if m < 4:
+                    rows = right[pl.ds(pl.multiple_of(half * ROWS + m * 256, 256), 256), :]
+                else:
+                    rows = lower[(m - 4) * 256 : (m - 3) * 256, :]
+                found = contract_lanes(rows, columns)
+                if first:
+                    acc[n, m * 256 : (m + 1) * 256, :] = found
+                else:
+                    acc[n, m * 256 : (m + 1) * 256, :] += found
             return carry
 
-        lax.fori_loop(0, 8, tile, 0)
-
-    def out_copy(n, slot):
-        columns = pl.ds(pl.multiple_of(n * 256, 256), 256)
-        return pltpu.make_async_copy(stage.at[slot], out_hbm.at[:, columns], out_sem.at[slot])
-
-    def finish():
-        def tile(n, carry):
-            slot = n % 2
-
-            @pl.when(n >= 2)
-            def _():
-                out_copy(n - 2, slot).wait()
-
-            columns = right[pl.ds(pl.multiple_of(n * 256, 256), 256), :]
-            for m in range(4):
-                rows = slice(m * 512, (m + 1) * 512)
-                total = acc[n, rows, :] + contract_lanes(left[rows, :], columns)
-                stage[slot, rows, :] = (total * (1.0 / 1024.0)).astype(BF)
-            out_copy(n, slot).start()
-            return carry
-
-        lax.fori_loop(0, 8, tile, 0)
-        out_copy(6, 0).wait()
-        out_copy(7, 1).wait()
+        lax.fori_loop(0, 2, tile, 0)
 
     def own_half(q):
         wait_slab(q, 0)
@@ -314,13 +314,12 @@
         for s in range(2):
             same = antenna == assign[:, s * ROWS : (s + 1) * ROWS]
             onehot[s, rows, :] = jnp.where(same, 1.0, 0.0).astype(BF)
-        acc[t] = jnp.zeros((INPUTS, 256), F32)
         return carry
 
     lax.fori_loop(0, 8, fill, 0)
     forward(1)
     own_half(0)
-    correlate()
+    correlate(True)
     other_half(0)
     correlate()
     forward(2)
@@ -336,8 +335,10 @@
     lax.fori_loop(1, 3, middle, 0)
     own_half(3)
     correlate()
-    other_half(3)
-    finish()
+    wait_slab(3, 1)
+    reorder_first(slab_b.at[3])
+    wait_slab(3, 2)
+    reorder_second(slab_c.at[3])
 
     for q in range(PARTS):
         sent = sendbuf.at[q, :, pl.ds(0, 31)]
@@ -346,35 +347,72 @@
             pltpu.make_async_copy(slab.at[q], slab.at[q], slab_send.at[q]).wait()
 
 
-def place_kernel(perm, x, o):
-    def body(g, carry):
-        rows = pl.ds(pl.multiple_of(g * 16, 16), 16)
+def finish_kernel(perm, acc, right, out_hbm, stage, out_sem):
+    half = lax.axis_index("tm")
+
+    def out_copy(t):
+        rows = pl.ds(pl.multiple_of(t * 128, 128), 128)
+        return pltpu.make_async_copy(stage.at[t % 2], out_hbm.at[rows], out_sem.at[t % 2])
+
+    def tile(t, carry):
+        slot = t % 2
+
+        @pl.when(t >= 2)
+        def _():
+            out_copy(t - 2).wait()
+
+        block = right[pl.ds(pl.multiple_of(half * ROWS + t * 128, 128), 128), :]
+        turned = jnp.concatenate([block[:, CHUNK:], -block[:, :CHUNK]], axis=1)
+        rows = jnp.concatenate([block, turned], axis=0)
         for jh in range(2):
-            parts = [
-                x[p, rows, (jh * 8 + j) * 128 : (jh * 8 + j + 1) * 128]
-                for j in range(8)
-                for p in range(2)
-            ]
-            moved = dot(perm[...], jnp.concatenate(parts, axis=0)).astype(BF)
-            o[rows, jh * 16 : (jh + 1) * 16, :] = moved.reshape(16, 16, 128)
+            found = contract_lanes(rows, right[jh * ROWS : (jh + 1) * ROWS, :])
+            pair = []
+            for p in range(2):
+                before = acc[jh, pl.ds(pl.multiple_of(p * ROWS + t * 128, 128), 128), :]
+                total = before + found[p * 128 : (p + 1) * 128]
+                pair.append((total * (1.0 / TOTAL_SPEC)).astype(BF))
+            for g in range(4):
+                sides = [
+                    jnp.concatenate(
+                        [
+                            pair[p][(2 * g + h) * 16 : (2 * g + h + 1) * 16, j * 128 : (j + 1) * 128]
+                            for j in range(8)
+                            for p in range(2)
+                        ],
+                        axis=0,
+                    )
+                    for h in range(2)
+                ]
+                moved = dot(perm[...], jnp.concatenate(sides, axis=1)).astype(BF)
+                for h in range(2):
+                    a = (2 * g + h) * 16
+                    stage[slot, a : a + 16, jh * 16 : (jh + 1) * 16, :] = moved[
+                        :, h * 128 : (h + 1) * 128
+                    ].reshape(16, 16, 128)
+        out_copy(t).start()
         return carry
 
-    lax.fori_loop(0, x.shape[1] // 16, body, 0)
+    lax.fori_loop(0, 8, tile, 0)
+    out_copy(6).wait()
+    out_copy(7).wait()
 
 
 def shards(voltages, kept, assign):
-    coef = coefficients(kept)
     dma = pltpu.SemaphoreType.DMA
     vmem = pl.BlockSpec(memory_space=pltpu.VMEM)
     hbm = pl.BlockSpec(memory_space=pl.ANY)
-    found = pl.pallas_call(
+    acc, right = pl.pallas_call(
         main_kernel,
-        out_shape=jax.ShapeDtypeStruct((2 * ROWS, INPUTS), BF),
-        in_specs=[hbm, vmem, vmem],
-        out_specs=hbm,
+        out_shape=[
+            pltpu.VMEM((2, 2 * ROWS, INPUTS // 2), F32),
+            pltpu.VMEM((INPUTS, WIDE), BF),
+        ],
+        in_specs=[hbm, vmem, vmem, vmem],
+        out_specs=[vmem, vmem],
         scratch_shapes=[
             pltpu.VMEM((LOCAL, SAMP_DEV), BF),
             pltpu.VMEM((256, 256), BF),
+            pltpu.VMEM((2 * CHANNELS, TAPS * NFFT), BF),
             pltpu.VMEM((16, CHUNK, 4 * NFFT), BF),
             pltpu.VMEM((16, CHANNELS, WIDE), BF),
             pltpu.VMEM((PARTS, 2, 32, LOCAL, WIDE), BF),
@@ -383,39 +421,36 @@
             pltpu.VMEM((PARTS, ROWS, WIDE), BF),
             pltpu.VMEM((PARTS, ROWS, WIDE), BF),
             pltpu.VMEM((2, INPUTS, ROWS), BF),
-            pltpu.VMEM((INPUTS, WIDE), BF),
-            pltpu.VMEM((2 * ROWS, WIDE), BF),
-            pltpu.VMEM((8, 2 * ROWS, 256), F32),
-            pltpu.VMEM((2, 2 * ROWS, 256), BF),
+            pltpu.VMEM((ROWS, WIDE), BF),
+            pltpu.VMEM((INPUTS, WIDE), F32),
             dma((PARTS,)),
             dma((PARTS,)),
             dma((PARTS, 4)),
             dma((PARTS,)),
             dma((PARTS, 3)),
-            dma((2,)),
         ],
         compiler_params=pltpu.CompilerParams(
-            collective_id=0, has_side_effects=True, vmem_limit_bytes=60 << 20
+            collective_id=0, has_side_effects=True, vmem_limit_bytes=42 << 20
         ),
         name="exchange_correlate",
-    )(voltages, coef, assign.reshape(1, INPUTS))
+    )(voltages, kept.reshape(1, CHANNELS), jnp.asarray(filter_window(), F32), assign.reshape(1, INPUTS))
 
     r = np.arange(256)
     source = ((r % 16) // 2) * 32 + (r % 2) * 16 + r // 16
     perm = jnp.asarray(source[:, None] == r[None, :], BF)
-    tile = 128
     placed = pl.pallas_call(
-        place_kernel,
-        grid=(ROWS // tile,),
-        in_specs=[
-            pl.BlockSpec((256, 256), lambda i: (0, 0)),
-            pl.BlockSpec((2, tile, INPUTS), lambda i: (0, i, 0)),
-        ],
-        out_specs=pl.BlockSpec((tile, 32, 128), lambda i: (i, 0, 0)),
+        finish_kernel,
+        in_specs=[vmem, vmem, vmem],
+        out_specs=hbm,
         out_shape=jax.ShapeDtypeStruct((ROWS, 32, 128), BF),
-        compiler_params=pltpu.CompilerParams(vmem_limit_bytes=16 << 20),
-        name="place",
-    )(perm, found.reshape(2, ROWS, INPUTS))
+        scratch_shapes=[pltpu.VMEM((2, 128, 32, 128), BF), dma((2,))],
+        compiler_params=pltpu.CompilerParams(vmem_limit_bytes=42 << 20),
+        name="finish",
+    )(
+        perm,
+        pltpu.with_memory_space_constraint(acc, pltpu.VMEM),
+        pltpu.with_memory_space_constraint(right, pltpu.VMEM),
+    )
     return placed.reshape(ROWS, 16, 2, 128).transpose(0, 2, 1, 3).reshape(1, ROWS, 2, INPUTS)
 
 

time: 160 us -> 127 us (0.79)
  Pallas kernels: 151 us -> 125 us
  local copies, waits for them, and re-layouts: 3.54 us -> 0 us
  other arithmetic: 3.12 us -> 0 us
    pallas_call x2, Pallas kernels: 151 us -> 125 us  [the longest x1 115 us: shards(): pl.pallas_call(main_kernel, out_shape=[pltpu.VMEM((2, 2 * ROWS, INPUTS //...]
    unnamed x4 -> x0, local copies, waits for them, and re-layouts: 3.38 us -> none
    convert_element_type x1 -> x0, other arithmetic: 2.39 us -> none  [coefficients(): return (jnp.cos(angles) * window).astype(BF).reshape(2 * CHANNELS, length)]
where the time goes in v2:
time: 127 us; the launch traced here: 125 us
  Pallas kernels  125 us (98%)
    pallas_call x1, Pallas kernels, shards(): pl.pallas_call(main_kernel, out_shape=[pltpu.VMEM((2, 2 * ROWS, INPUTS //...  115 us
    pallas_call x1, Pallas kernels, shards(): pl.pallas_call(finish_kernel, in_specs=[vmem, vmem, vmem], out_specs=hbm,...  9.89 us

profile of v2, /device:TPU:1, one launch (start us, length us, event | category | flops | bytes accessed | tf_op | source)
XLA Modules:
  0.0 125.1 jit_solution(9244170283258180226)
XLA Ops:
  0.0 115.0 %exchange_correlate.1 = (f32[2,2048,1024]{2,1,0:T(8,128)S(1)}, bf16[2048,256]{1,0:T(8,128)(2,1)S(1)}) custom-call(bf16[32,65920]{1,0:T(8,128)(2,1)} %volt_hbm.1, s32[1,64]{1,0:T(1,128)} %bitcast.8, f32[1,512]{1,0:T(1,128)} %constant.4.clone.window, s32[1,2048]{1,0:T(1,128)} %bitcast.7), custom_call_target="tpu_custom_call" | custom-call | tf_op jit(solution)/shard_map/exchange_correlate/pallas_call | solution.py:404
  115.0 9.9 %finish.1 = bf16[1024,32,128]{2,1,0:T(8,128)(2,1)} custom-call(bf16[256,256]{1,0:T(8,128)(2,1)} %constant.5.clone.perm, f32[2,2048,1024]{2,1,0:T(8,128)S(1)} %get-tuple-element.7.acc, bf16[2048,256]{1,0:T(8,128)(2,1)S(1)} %get-tuple-element.8.right), custom_call_target="tpu_custom_call" | custom-call | tf_op jit(solution)/shard_map/finish/pallas_call | solution.py:441

commit v3 on v2

--- a/solution.py
+++ b/solution.py
@@ -63,6 +63,9 @@
     near_recv,
     slab_send,
     slab_recv,
+    last_recv,
+    crossed,
+    cross_recv,
 ):
     me = lax.axis_index("chan")
     half = lax.axis_index("tm")
@@ -78,8 +81,7 @@
         part = pl.ds(first, last - first)
         return pltpu.make_async_copy(volt_hbm.at[:, part], volt.at[:, part], volt_sem.at[q])
 
-    for q in range(PARTS):
-        volt_copy(q).start()
+    volt_copy(0).start()
 
     def near_device(dy, dz, dc):
         there = (((y + dy) % 4) * 4 + (z + dz) % 4) * 2 + (core + dc) % 2
@@ -122,6 +124,9 @@
 
     def channelize(q):
         volt_copy(q).wait()
+        if q == 0:
+            for later in range(1, PARTS):
+                volt_copy(later).start()
         for ih in range(2):
 
             def reorder(sb, carry):
@@ -171,45 +176,64 @@
             device_id_type=MESH,
         )
 
-    def send_near(q):
-        self_copy(q).start()
-        if q == 0:
-
-            def first(k, carry):
-                near_copy(q, 0, k // 2, k % 2).start()
-                return carry
-
-            lax.fori_loop(1, 8, first, 0)
-
-            def second(k, carry):
-                near_copy(q, 1 + 2 * (k % 2), (k // 2) % 4, k // 8).start()
-                return carry
-
-            lax.fori_loop(0, 16, second, 0)
-
-            def third(k, carry):
-                near_copy(q, 2, k // 2, k % 2).start()
-                return carry
-
-            lax.fori_loop(0, 8, third, 0)
+    def cross_copy(piece, kind):
+        which = low if kind == 2 else 1 - low
+        blocks = slice(piece * 8, piece * 8 + 8)
+        return pltpu.make_async_remote_copy(
+            src_ref=sendbuf.at[0, which, blocks],
+            dst_ref=crossed.at[kind, blocks],
+            send_sem=slab_send.at[0],
+            recv_sem=cross_recv.at[kind],
+            device_id=far[kind],
+            device_id_type=MESH,
+        )
+
+    def spread(kind):
+        if kind == 3:
+            source, target, sem = sendbuf.at[0, low], near.at[0, low], near_recv.at[0, 0]
         else:
-
-            def some(k, carry):
-                o = (k * 11) % 32
-                near_copy(q, o % 4, (o // 4) % 4, o // 16).start()
-                return carry
-
-            lax.fori_loop(1, 32, some, 0)
+            block = crossed.at[kind]
+            pltpu.make_async_copy(block, block, cross_recv.at[kind]).wait()
+            source, target = block, (slab_a, slab_b, slab_c)[kind].at[0]
+            sem = slab_recv.at[0, kind]
+        pltpu.make_async_copy(source.at[place], target.at[my_rows], sem).start()
+
+        def some(k, carry):
+            o = (k * 11) % 32
+            there = near_device(o % 4, (o // 4) % 4, o // 16)
+            pltpu.make_async_remote_copy(
+                src_ref=source.at[there],
+                dst_ref=target.at[my_rows],
+                send_sem=near_send.at[0],
+                recv_sem=sem,
+                device_id=(low * 32 + there, half),
+                device_id_type=MESH,
+            ).start()
+            return carry
+
+        lax.fori_loop(1, 32, some, 0)
+
+    def some_near(q, first, last):
+        if first == 1:
+            self_copy(q).start()
+
+        def some(k, carry):
+            o = (k * 11) % 32
+            near_copy(q, o % 4, (o // 4) % 4, o // 16).start()
+            return carry
+
+        lax.fori_loop(first, last, some, 0)
 
     def slab_copy(q, group, kind):
         rows = pl.ds(pl.multiple_of(group * 256, 256), 256)
         which = low if kind == 2 else 1 - low
         slab = (slab_a, slab_b, slab_c)[kind]
+        last = q == PARTS - 1 and kind == 2
         return pltpu.make_async_remote_copy(
             src_ref=near.at[q, which, rows],
             dst_ref=slab.at[q, rows],
             send_sem=slab_send.at[q],
-            recv_sem=slab_recv.at[q, kind],
+            recv_sem=last_recv.at[group] if last else slab_recv.at[q, kind],
             device_id=far[kind],
             device_id_type=MESH,
         )
@@ -218,12 +242,6 @@
         rows = pl.ds(pl.multiple_of(group * 256, 256), 256)
         block = near.at[q, :, rows]
         pltpu.make_async_copy(block, block, near_recv.at[q, group]).wait()
-
-    def forward_group(q, step):
-        group = (y + (0, 1, 3, 2)[step]) % 4
-        wait_group(q, group)
-        for kind in range(3):
-            slab_copy(q, group, kind).start()
 
     def forward(q):
         for step in range(4):
@@ -255,14 +273,18 @@
 
         lax.fori_loop(0, 2, part, 0)
 
-    def reorder_second(mine):
-        def part(t, carry):
-            rows = pl.ds(pl.multiple_of(t * 1024, 1024), 1024)
-            total = partial[rows, :] + dot(onehot[low, rows, :], mine[...])
-            right[rows, :] = total.astype(BF)
-            return carry
-
-        lax.fori_loop(0, 2, part, 0)
+    def reorder_second(q):
+        for group in range(4):
+            inputs = slice(group * 256, (group + 1) * 256)
+            block = slab_c.at[q, inputs]
+            pltpu.make_async_copy(block, block, last_recv.at[group]).wait()
+            for t in range(2):
+                rows = slice(t * 1024, (t + 1) * 1024)
+                total = partial[rows, :] + dot(onehot[low, rows, inputs], slab_c[q, inputs, :])
+                if group == 3:
+                    right[rows, :] = total.astype(BF)
+                else:
+                    partial[rows, :] = total
 
     def correlate(first=False):
         for t in range(4):
@@ -288,6 +310,9 @@
 
     def own_half(q):
         wait_slab(q, 0)
+        if q == 0:
+            block = near.at[0, low]
+            pltpu.make_async_copy(block, block, near_recv.at[0, 0]).wait()
         reorder_inputs(near.at[q, low], slab_a.at[q])
 
     def other_half(q):
@@ -297,16 +322,15 @@
 
     channelize(0)
     pl.semaphore_wait(barrier, 34)
-    send_near(0)
-    forward_group(0, 0)
+    for piece in range(4):
+        for kind in range(3):
+            cross_copy(piece, kind).start()
     channelize(1)
-    send_near(1)
-    for step in range(1, 4):
-        forward_group(0, step)
+    some_near(1, 1, 32)
+    spread(3)
     channelize(2)
-    send_near(2)
+    some_near(2, 1, 32)
     channelize(3)
-    send_near(3)
 
     def fill(t, carry):
         rows = pl.ds(pl.multiple_of(t * 256, 256), 256)
@@ -318,31 +342,30 @@
 
     lax.fori_loop(0, 8, fill, 0)
     forward(1)
-    own_half(0)
+    for kind in range(3):
+        spread(kind)
+    some_near(3, 1, 32)
+    forward(2)
+    own_half(1)
     correlate(True)
-    other_half(0)
+    other_half(1)
     correlate()
-    forward(2)
     forward(3)
-
-    def middle(q, carry):
+    for q in (0, 2):
         own_half(q)
         correlate()
         other_half(q)
         correlate()
-        return carry
-
-    lax.fori_loop(1, 3, middle, 0)
     own_half(3)
     correlate()
     wait_slab(3, 1)
     reorder_first(slab_b.at[3])
-    wait_slab(3, 2)
-    reorder_second(slab_c.at[3])
+    reorder_second(3)
 
     for q in range(PARTS):
         sent = sendbuf.at[q, :, pl.ds(0, 31)]
-        pltpu.make_async_copy(sent, sent, near_send.at[q]).wait()
+        for _ in range(2 if q == 0 else 1):
+            pltpu.make_async_copy(sent, sent, near_send.at[q]).wait()
         for slab in (slab_a, slab_b, slab_c):
             pltpu.make_async_copy(slab.at[q], slab.at[q], slab_send.at[q]).wait()
 
@@ -351,27 +374,20 @@
     half = lax.axis_index("tm")
 
     def out_copy(t):
-        rows = pl.ds(pl.multiple_of(t * 128, 128), 128)
-        return pltpu.make_async_copy(stage.at[t % 2], out_hbm.at[rows], out_sem.at[t % 2])
-
-    def tile(t, carry):
-        slot = t % 2
-
-        @pl.when(t >= 2)
-        def _():
-            out_copy(t - 2).wait()
-
-        block = right[pl.ds(pl.multiple_of(half * ROWS + t * 128, 128), 128), :]
+        return pltpu.make_async_copy(stage.at[t], out_hbm.at[t * 256 : (t + 1) * 256], out_sem.at[t])
+
+    for t in range(4):
+        block = right[pl.ds(pl.multiple_of(half * ROWS + t * 256, 256), 256), :]
         turned = jnp.concatenate([block[:, CHUNK:], -block[:, :CHUNK]], axis=1)
         rows = jnp.concatenate([block, turned], axis=0)
         for jh in range(2):
             found = contract_lanes(rows, right[jh * ROWS : (jh + 1) * ROWS, :])
             pair = []
             for p in range(2):
-                before = acc[jh, pl.ds(pl.multiple_of(p * ROWS + t * 128, 128), 128), :]
-                total = before + found[p * 128 : (p + 1) * 128]
-                pair.append((total * (1.0 / TOTAL_SPEC)).astype(BF))
-            for g in range(4):
+                first = p * ROWS + t * 256
+                total = acc[jh, first : first + 256, :] + found[p * 256 : (p + 1) * 256]
+                pair.append(total.astype(BF))
+            for g in range(8):
                 sides = [
                     jnp.concatenate(
                         [
@@ -386,15 +402,12 @@
                 moved = dot(perm[...], jnp.concatenate(sides, axis=1)).astype(BF)
                 for h in range(2):
                     a = (2 * g + h) * 16
-                    stage[slot, a : a + 16, jh * 16 : (jh + 1) * 16, :] = moved[
+                    stage[t, a : a + 16, jh * 16 : (jh + 1) * 16, :] = moved[
                         :, h * 128 : (h + 1) * 128
                     ].reshape(16, 16, 128)
         out_copy(t).start()
-        return carry
-
-    lax.fori_loop(0, 8, tile, 0)
-    out_copy(6).wait()
-    out_copy(7).wait()
+    for t in range(4):
+        out_copy(t).wait()
 
 
 def shards(voltages, kept, assign):
@@ -428,6 +441,9 @@
             dma((PARTS, 4)),
             dma((PARTS,)),
             dma((PARTS, 3)),
+            dma((4,)),
+            pltpu.VMEM((3, 32, LOCAL, WIDE), BF),
+            dma((3,)),
         ],
         compiler_params=pltpu.CompilerParams(
             collective_id=0, has_side_effects=True, vmem_limit_bytes=42 << 20
@@ -437,13 +453,13 @@
 
     r = np.arange(256)
     source = ((r % 16) // 2) * 32 + (r % 2) * 16 + r // 16
-    perm = jnp.asarray(source[:, None] == r[None, :], BF)
+    perm = jnp.asarray((source[:, None] == r[None, :]) / TOTAL_SPEC, BF)
     placed = pl.pallas_call(
         finish_kernel,
         in_specs=[vmem, vmem, vmem],
         out_specs=hbm,
         out_shape=jax.ShapeDtypeStruct((ROWS, 32, 128), BF),
-        scratch_shapes=[pltpu.VMEM((2, 128, 32, 128), BF), dma((2,))],
+        scratch_shapes=[pltpu.VMEM((4, 256, 32, 128), BF), dma((4,))],
         compiler_params=pltpu.CompilerParams(vmem_limit_bytes=42 << 20),
         name="finish",
     )(

time: 127 us -> 111 us (0.87); the launches traced: 125 us -> 111 us
  Pallas kernels: 125 us -> 111 us
    pallas_call x1, Pallas kernels: 115 us -> 103 us  [shards(): pl.pallas_call(main_kernel, out_shape=[pltpu.VMEM((2, 2 * ROWS, INPUTS //...]
    pallas_call x1, Pallas kernels: 9.89 us -> 7.54 us  [shards(): pl.pallas_call(finish_kernel, in_specs=[vmem, vmem, vmem], out_specs=hbm,...]
where the time goes in v3:
time: 111 us
  Pallas kernels  111 us (100%)
    pallas_call x1, Pallas kernels, shards(): pl.pallas_call(main_kernel, out_shape=[pltpu.VMEM((2, 2 * ROWS, INPUTS //...  103 us
    pallas_call x1, Pallas kernels, shards(): pl.pallas_call(finish_kernel, in_specs=[vmem, vmem, vmem], out_specs=hbm,...  7.54 us

profile of v3, /device:TPU:1, one launch (start us, length us, event | category | flops | bytes accessed | tf_op | source)
XLA Modules:
  0.0 110.9 jit_solution(9797206168649350118)
XLA Ops:
  0.0 103.2 %exchange_correlate.1 = (f32[2,2048,1024]{2,1,0:T(8,128)S(1)}, bf16[2048,256]{1,0:T(8,128)(2,1)S(1)}) custom-call(bf16[32,65920]{1,0:T(8,128)(2,1)} %volt_hbm.1, s32[1,64]{1,0:T(1,128)} %bitcast.8, f32[1,512]{1,0:T(1,128)} %constant.4.clone.window, s32[1,2048]{1,0:T(1,128)} %bitcast.7), custom_call_target="tpu_custom_call" | custom-call | tf_op jit(solution)/shard_map/exchange_correlate/pallas_call | solution.py:417
  103.2 7.5 %finish.1 = bf16[1024,32,128]{2,1,0:T(8,128)(2,1)} custom-call(bf16[256,256]{1,0:T(8,128)(2,1)} %constant.5.clone.perm, f32[2,2048,1024]{2,1,0:T(8,128)S(1)} %get-tuple-element.7.acc, bf16[2048,256]{1,0:T(8,128)(2,1)S(1)} %get-tuple-element.8.right), custom_call_target="tpu_custom_call" | custom-call | tf_op jit(solution)/shard_map/finish/pallas_call | solution.py:457

commit v4 on v3

--- a/solution.py
+++ b/solution.py
@@ -370,43 +370,34 @@
             pltpu.make_async_copy(slab.at[q], slab.at[q], slab_send.at[q]).wait()
 
 
-def finish_kernel(perm, acc, right, out_hbm, stage, out_sem):
+TILE = 128
+STEP = 36
+
+
+def finish_kernel(acc, right, out_hbm, wide, stage, out_sem):
     half = lax.axis_index("tm")
 
     def out_copy(t):
-        return pltpu.make_async_copy(stage.at[t], out_hbm.at[t * 256 : (t + 1) * 256], out_sem.at[t])
-
-    for t in range(4):
-        block = right[pl.ds(pl.multiple_of(half * ROWS + t * 256, 256), 256), :]
+        return pltpu.make_async_copy(
+            stage.at[t], out_hbm.at[t * TILE : (t + 1) * TILE], out_sem.at[t]
+        )
+
+    for t in range(ROWS // TILE):
+        block = right[pl.ds(pl.multiple_of(half * ROWS + t * TILE, TILE), TILE), :]
         turned = jnp.concatenate([block[:, CHUNK:], -block[:, :CHUNK]], axis=1)
         rows = jnp.concatenate([block, turned], axis=0)
         for jh in range(2):
             found = contract_lanes(rows, right[jh * ROWS : (jh + 1) * ROWS, :])
-            pair = []
             for p in range(2):
-                first = p * ROWS + t * 256
-                total = acc[jh, first : first + 256, :] + found[p * 256 : (p + 1) * 256]
-                pair.append(total.astype(BF))
-            for g in range(8):
-                sides = [
-                    jnp.concatenate(
-                        [
-                            pair[p][(2 * g + h) * 16 : (2 * g + h + 1) * 16, j * 128 : (j + 1) * 128]
-                            for j in range(8)
-                            for p in range(2)
-                        ],
-                        axis=0,
-                    )
-                    for h in range(2)
-                ]
-                moved = dot(perm[...], jnp.concatenate(sides, axis=1)).astype(BF)
-                for h in range(2):
-                    a = (2 * g + h) * 16
-                    stage[t, a : a + 16, jh * 16 : (jh + 1) * 16, :] = moved[
-                        :, h * 128 : (h + 1) * 128
-                    ].reshape(16, 16, 128)
+                first = p * ROWS + t * TILE
+                total = acc[jh, first : first + TILE, :] + found[p * TILE : (p + 1) * TILE]
+                for j in range(8):
+                    place = pl.ds(2 * (jh * 8 + j) + p, TILE, stride=STEP)
+                    wide[t % 2, place, :] = total[:, j * 128 : (j + 1) * 128]
+        for a in range(TILE):
+            stage[t, a] = (wide[t % 2, a * STEP : a * STEP + 32, :] * (1.0 / TOTAL_SPEC)).astype(BF)
         out_copy(t).start()
-    for t in range(4):
+    for t in range(ROWS // TILE):
         out_copy(t).wait()
 
 
@@ -451,19 +442,19 @@
         name="exchange_correlate",
     )(voltages, kept.reshape(1, CHANNELS), jnp.asarray(filter_window(), F32), assign.reshape(1, INPUTS))
 
-    r = np.arange(256)
-    source = ((r % 16) // 2) * 32 + (r % 2) * 16 + r // 16
-    perm = jnp.asarray((source[:, None] == r[None, :]) / TOTAL_SPEC, BF)
     placed = pl.pallas_call(
         finish_kernel,
-        in_specs=[vmem, vmem, vmem],
+        in_specs=[vmem, vmem],
         out_specs=hbm,
         out_shape=jax.ShapeDtypeStruct((ROWS, 32, 128), BF),
-        scratch_shapes=[pltpu.VMEM((4, 256, 32, 128), BF), dma((4,))],
+        scratch_shapes=[
+            pltpu.VMEM((2, TILE * STEP, 128), F32),
+            pltpu.VMEM((ROWS // TILE, TILE, 32, 128), BF),
+            dma((ROWS // TILE,)),
+        ],
         compiler_params=pltpu.CompilerParams(vmem_limit_bytes=42 << 20),
         name="finish",
     )(
-        perm,
         pltpu.with_memory_space_constraint(acc, pltpu.VMEM),
         pltpu.with_memory_space_constraint(right, pltpu.VMEM),
     )

time: 111 us -> 108 us (0.973)
  Pallas kernels: 111 us -> 108 us
    pallas_call x1, Pallas kernels: 7.54 us -> 4.69 us  [shards(): pl.pallas_call(finish_kernel, in_specs=[vmem, vmem], out_specs=hbm, out_s...]
where the time goes in v4:
time: 108 us
  Pallas kernels  108 us (100%)
    pallas_call x1, Pallas kernels, shards(): pl.pallas_call(main_kernel, out_shape=[pltpu.VMEM((2, 2 * ROWS, INPUTS //...  103 us
    pallas_call x1, Pallas kernels, shards(): pl.pallas_call(finish_kernel, in_specs=[vmem, vmem], out_specs=hbm, out_s...  4.69 us

profile of v4, /device:TPU:1, one launch (start us, length us, event | category | flops | bytes accessed | tf_op | source)
XLA Modules:
  0.0 108.1 jit_solution(532773335722196707)
XLA Ops:
  0.0 103.2 %exchange_correlate.1 = (f32[2,2048,1024]{2,1,0:T(8,128)S(1)}, bf16[2048,256]{1,0:T(8,128)(2,1)S(1)}) custom-call(bf16[32,65920]{1,0:T(8,128)(2,1)} %volt_hbm.1, s32[1,64]{1,0:T(1,128)} %bitcast.8, f32[1,512]{1,0:T(1,128)} %constant.2.clone.window, s32[1,2048]{1,0:T(1,128)} %bitcast.7), custom_call_target="tpu_custom_call" | custom-call | tf_op jit(solution)/shard_map/exchange_correlate/pallas_call | solution.py:408
  103.2 4.7 %finish.1 = bf16[1024,32,128]{2,1,0:T(8,128)(2,1)} custom-call(f32[2,2048,1024]{2,1,0:T(8,128)S(1)} %get-tuple-element.7.acc, bf16[2048,256]{1,0:T(8,128)(2,1)S(1)} %get-tuple-element.8.right), custom_call_target="tpu_custom_call" | custom-call | tf_op jit(solution)/shard_map/finish/pallas_call | solution.py:445

commit v5 on v4

--- a/solution.py
+++ b/solution.py
@@ -224,8 +224,9 @@
 
         lax.fori_loop(first, last, some, 0)
 
-    def slab_copy(q, group, kind):
-        rows = pl.ds(pl.multiple_of(group * 256, 256), 256)
+    def slab_copy(q, piece, kind):
+        rows = pl.ds(piece * 128, 128)
+        group = piece // 2
         which = low if kind == 2 else 1 - low
         slab = (slab_a, slab_b, slab_c)[kind]
         last = q == PARTS - 1 and kind == 2
@@ -246,11 +247,11 @@
     def forward(q):
         for step in range(4):
             wait_group(q, (y + step) % 4)
-        for step in range(4):
+        for piece in range(8):
             for kind in range(2):
-                slab_copy(q, step, kind).start()
-        for step in range(4):
-            slab_copy(q, step, 2).start()
+                slab_copy(q, piece, kind).start()
+        for piece in range(8):
+            slab_copy(q, piece, 2).start()
 
     def wait_slab(q, kind):
         block = (slab_a, slab_b, slab_c)[kind].at[q]

time: 108 us -> 108 us (level)
  no operation moved by 1% of the time
where the time goes in v5:
time: 108 us
  Pallas kernels  108 us (100%)
    pallas_call x1, Pallas kernels, shards(): pl.pallas_call(main_kernel, out_shape=[pltpu.VMEM((2, 2 * ROWS, INPUTS //...  103 us
    pallas_call x1, Pallas kernels, shards(): pl.pallas_call(finish_kernel, in_specs=[vmem, vmem], out_specs=hbm, out_s...  4.69 us

profile of v5, /device:TPU:1, one launch (start us, length us, event | category | flops | bytes accessed | tf_op | source)
XLA Modules:
  0.0 108.1 jit_solution(10060742760939078904)
XLA Ops:
  0.0 103.2 %exchange_correlate.1 = (f32[2,2048,1024]{2,1,0:T(8,128)S(1)}, bf16[2048,256]{1,0:T(8,128)(2,1)S(1)}) custom-call(bf16[32,65920]{1,0:T(8,128)(2,1)} %volt_hbm.1, s32[1,64]{1,0:T(1,128)} %bitcast.8, f32[1,512]{1,0:T(1,128)} %constant.2.clone.window, s32[1,2048]{1,0:T(1,128)} %bitcast.7), custom_call_target="tpu_custom_call" | custom-call | tf_op jit(solution)/shard_map/exchange_correlate/pallas_call | solution.py:409
  103.2 4.7 %finish.1 = bf16[1024,32,128]{2,1,0:T(8,128)(2,1)} custom-call(f32[2,2048,1024]{2,1,0:T(8,128)S(1)} %get-tuple-element.7.acc, bf16[2048,256]{1,0:T(8,128)(2,1)S(1)} %get-tuple-element.8.right), custom_call_target="tpu_custom_call" | custom-call | tf_op jit(solution)/shard_map/finish/pallas_call | solution.py:446
